TPU v7x, 32 devices: a whole 2x2x4 slice. The times are simulated.
32 devices in a mesh: dom: 8 (over z, y), sub: 4 (over x, core).
Axes of the slice: x: 2, y: 2, z: 4, core: 2. Of those that a mesh axis runs over, the one named last changes fastest.
Arguments:
- rhs: float32 [5, 64, 4096], P(None, 'sub', 'dom'), may hold values from -0.4 to 0.4
- lateral: float32 [5, 64, 4096], P(None, 'sub', 'dom'), may hold values from 0.05 to 0.5
- piece_line: int32 [4, 4096], P('sub', 'dom'), may hold values from 0 to 4095, as said below
- lower: float32 [5, 5, 64, 4096], P(None, None, None, ('dom', 'sub'))
- diag_blocks: float32 [5, 5, 64, 4096], P(None, None, None, ('dom', 'sub')), as said below
- upper: float32 [5, 5, 64, 4096], P(None, None, None, ('dom', 'sub'))
Outputs:
- correction: float32 [5, 64, 4096], P(None, 'sub', 'dom')
Inputs may be any that keep to these rules, and one draw needn't show every extreme that they name: For each s, piece_line[s] holds every line id once. The owner of a line is line // 512; the 512 slots of one index of dom hold at most 96 pieces of one owner's lines, and some hold exactly 96. Every block row of the three arrays is diagonally dominant: the diagonal entry of diag_blocks exceeds the sum of magnitudes of the other entries of its row in all three.
All inputs are finite; a program needn't handle non-finite values.
Results may differ from a plain program's by a relative error of at most 0.00002.
Values sent between devices are 32-bit elements; how exact they have to be, the bound alone decides.
A program may use at most 64 MiB of HBM per device.

v0:
```python
import functools

import jax
import jax.numpy as jnp
from jax import lax
from jax.experimental import pallas as pl
from jax.experimental.pallas import tpu as pltpu
from jax.sharding import PartitionSpec as P

F = 5
VMEM = pl.BlockSpec(memory_space=pltpu.VMEM)
PARAMS = pltpu.CompilerParams(vmem_limit_bytes=40 * 1024 * 1024)
NT = (((1,), (1,)), ((), ()))
NN = (((1,), (0,)), ((), ()))


def dot(left, right, dims):
    return lax.dot_general(
        left, right, dims, precision=lax.Precision.HIGHEST, preferred_element_type=jnp.float32
    )


def call(kernel, outs, *args, scratch=()):
    return pl.pallas_call(
        kernel,
        out_shape=outs,
        in_specs=[VMEM] * len(args),
        out_specs=jax.tree.map(lambda _: VMEM, outs),
        scratch_shapes=list(scratch),
        compiler_params=PARAMS,
    )(*args)


def load(ref, rows):
    return [[ref[i, j, rows, :] for j in range(F)] for i in range(F)]


def save(ref, rows, matrix):
    for i in range(F):
        for j in range(F):
            ref[i, j, rows, :] = matrix[i][j]


def total(terms):
    out = terms[0]
    for term in terms[1:]:
        out = lax.add(out, term)
    return out


def mul(left, right):
    return [
        [total([lax.mul(left[i][k], right[k][j]) for k in range(F)]) for j in range(F)]
        for i in range(F)
    ]


def mulvec(left, vector):
    return [total([lax.mul(left[i][k], vector[k]) for k in range(F)]) for i in range(F)]


def neg(matrix):
    return [[lax.neg(e) for e in row] for row in matrix]


def plus(*matrices):
    return [[total([m[i][j] for m in matrices]) for j in range(F)] for i in range(F)]


def invert(matrix):
    a = [list(row) for row in matrix]
    one = jnp.ones_like(a[0][0])
    for k in range(F):
        pivot = one / a[k][k]
        a[k] = [pivot if j == k else lax.mul(a[k][j], pivot) for j in range(F)]
        for i in range(F):
            if i != k:
                f = a[i][k]
                a[i] = [
                    lax.neg(lax.mul(f, pivot)) if j == k else lax.sub(a[i][j], lax.mul(f, a[k][j]))
                    for j in range(F)
                ]
    return a


def levels_of(count):
    sizes, base = [], 0
    while count > 8:
        half = count // 2
        sizes.append((half, base))
        base += 5 * half
        count = half
    return sizes, base


def factor_kernel(low, mid, high, out, *scratch):
    count = low.shape[2]
    sizes, base = levels_of(count)
    depth = len(sizes)
    lows, mids, highs = scratch[:depth], scratch[depth : 2 * depth], scratch[2 * depth : 3 * depth]
    inv_buf, low_pad, inv_pad, high_pad = scratch[3 * depth :]
    for source, target in ((low, lows[0]), (mid, mids[0]), (high, highs[0])):
        target[:, :, :count, :] = source[...]
    for group in (lows, mids, highs):
        for buf in group:
            rows = buf.shape[2]
            buf[:, :, rows - 8 :, :] = jnp.zeros((F, F, 8, buf.shape[3]), jnp.float32)
    for buf in (low_pad, inv_pad, high_pad):
        buf[...] = jnp.zeros_like(buf)
    last = None
    for level, (half, at) in enumerate(sizes):
        lo, mi, hi = lows[level], mids[level], highs[level]
        inv_buf[:, :, half : half + 8, :] = jnp.zeros((F, F, 8, inv_buf.shape[3]), jnp.float32)
        for c in range(half // 8):
            inv = invert(load(mi, pl.ds(16 * c, 8, 2)))
            save(inv_buf, pl.ds(8 * c, 8), inv)
            save(out, pl.ds(at + 8 * c, 8), inv)
        for c in range(half // 8):
            inv = load(inv_buf, pl.ds(8 * c, 8))
            low_even = load(lo, pl.ds(16 * c, 8, 2))
            high_even = load(hi, pl.ds(16 * c, 8, 2))
            alpha = neg(mul(load(lo, pl.ds(16 * c + 1, 8, 2)), inv))
            save(out, pl.ds(at + half + 8 * c, 8), alpha)
            save(out, pl.ds(at + 3 * half + 8 * c, 8), low_even)
            save(out, pl.ds(at + 4 * half + 8 * c, 8), high_even)
            low_new = mul(alpha, low_even)
            mid_part = plus(load(mi, pl.ds(16 * c + 1, 8, 2)), mul(alpha, high_even))
            gamma = neg(mul(load(hi, pl.ds(16 * c + 1, 8, 2)), load(inv_buf, pl.ds(8 * c + 1, 8))))
            save(out, pl.ds(at + 2 * half + 8 * c, 8), gamma)
            mid_new = plus(mid_part, mul(gamma, load(lo, pl.ds(16 * c + 2, 8, 2))))
            high_new = mul(gamma, load(hi, pl.ds(16 * c + 2, 8, 2)))
            if level + 1 < depth:
                save(lows[level + 1], pl.ds(8 * c, 8), low_new)
                save(mids[level + 1], pl.ds(8 * c, 8), mid_new)
                save(highs[level + 1], pl.ds(8 * c, 8), high_new)
            else:
                last = (low_new, mid_new, high_new)
    lo, mi, hi = last
    for index, step in enumerate((1, 2, 4)):
        save(low_pad, pl.ds(8, 8), lo)
        save(high_pad, pl.ds(8, 8), hi)
        save(inv_pad, pl.ds(8, 8), invert(mi))
        below, above = pl.ds(8 - step, 8), pl.ds(8 + step, 8)
        alpha = neg(mul(lo, load(inv_pad, below)))
        gamma = neg(mul(hi, load(inv_pad, above)))
        save(out, pl.ds(base + 16 * index, 8), alpha)
        save(out, pl.ds(base + 16 * index + 8, 8), gamma)
        mi = plus(mi, mul(alpha, load(high_pad, below)), mul(gamma, load(low_pad, above)))
        lo = mul(alpha, load(low_pad, below))
        hi = mul(gamma, load(high_pad, above))
    save(out, pl.ds(base + 48, 8), invert(mi))


def factor(low, mid, high):
    count, lanes = low.shape[2:]
    sizes, base = levels_of(count)
    pads = [pltpu.VMEM((F, F, 2 * half + 8, lanes), jnp.float32) for half, _ in sizes]
    scratch = pads * 3 + [pltpu.VMEM((F, F, count // 2 + 8, lanes), jnp.float32)]
    scratch += [pltpu.VMEM((F, F, 24, lanes), jnp.float32)] * 3
    out = jax.ShapeDtypeStruct((F, F, base + 56, lanes), jnp.float32)
    return call(factor_kernel, out, low, mid, high, scratch=scratch)


def vload(ref, rows):
    return [ref[i, rows, :] for i in range(F)]


def vsave(ref, rows, vector):
    for i in range(F):
        ref[i, rows, :] = vector[i]


def vplus(*vectors):
    return [total([v[i] for v in vectors]) for i in range(F)]


def vminus(a, b):
    return [lax.sub(x, y) for x, y in zip(a, b)]


def solve_kernel(fac, given, out, *scratch):
    parts, rows, lanes = given.shape
    piece = rows // F
    sizes, base = levels_of(parts * piece)
    depth = len(sizes)
    vals, sols = scratch[:depth], scratch[depth : 2 * depth]
    pad, top = scratch[2 * depth :]
    for f in range(F):
        for s in range(parts):
            vals[0][f, s * piece : (s + 1) * piece, :] = given[s, f * piece : (f + 1) * piece, :]
    for buf in vals:
        buf[:, buf.shape[1] - 8 :, :] = jnp.zeros((F, 8, lanes), jnp.float32)
    for buf in tuple(sols) + (top,):
        buf[:, :8, :] = jnp.zeros((F, 8, lanes), jnp.float32)
    pad[...] = jnp.zeros_like(pad)
    value = None
    for level, (half, at) in enumerate(sizes):
        val = vals[level]
        for c in range(half // 8):
            value = vplus(
                vload(val, pl.ds(16 * c + 1, 8, 2)),
                mulvec(load(fac, pl.ds(at + half + 8 * c, 8)), vload(val, pl.ds(16 * c, 8, 2))),
                mulvec(load(fac, pl.ds(at + 2 * half + 8 * c, 8)), vload(val, pl.ds(16 * c + 2, 8, 2))),
            )
            if level + 1 < depth:
                vsave(vals[level + 1], pl.ds(8 * c, 8), value)
    for index, step in enumerate((1, 2, 4)):
        vsave(pad, pl.ds(8, 8), value)
        value = vplus(
            value,
            mulvec(load(fac, pl.ds(base + 16 * index, 8)), vload(pad, pl.ds(8 - step, 8))),
            mulvec(load(fac, pl.ds(base + 16 * index + 8, 8)), vload(pad, pl.ds(8 + step, 8))),
        )
    vsave(top, pl.ds(8, 8), mulvec(load(fac, pl.ds(base + 48, 8)), value))
    above = top
    for level in reversed(range(depth)):
        half, at = sizes[level]
        for c in range(half // 8):
            x_odd = vload(above, pl.ds(8 + 8 * c, 8))
            x_prev = vload(above, pl.ds(7 + 8 * c, 8))
            rest = vminus(
                vminus(
                    vload(vals[level], pl.ds(16 * c, 8, 2)),
                    mulvec(load(fac, pl.ds(at + 3 * half + 8 * c, 8)), x_prev),
                ),
                mulvec(load(fac, pl.ds(at + 4 * half + 8 * c, 8)), x_odd),
            )
            x_even = mulvec(load(fac, pl.ds(at + 8 * c, 8)), rest)
            vsave(sols[level], pl.ds(8 + 16 * c, 8, 2), x_even)
            vsave(sols[level], pl.ds(9 + 16 * c, 8, 2), x_odd)
        above = sols[level]
    for f in range(F):
        for s in range(parts):
            out[s, f * piece : (f + 1) * piece, :] = above[f, 8 + s * piece : 8 + (s + 1) * piece, :]


def solve(fac, given):
    parts, rows, lanes = given.shape
    sizes, _ = levels_of(parts * rows // F)
    pads = [pltpu.VMEM((F, 2 * half + 8, lanes), jnp.float32) for half, _ in sizes]
    scratch = pads * 2 + [pltpu.VMEM((F, 24, lanes), jnp.float32), pltpu.VMEM((F, 16, lanes), jnp.float32)]
    return call(solve_kernel, jax.ShapeDtypeStruct(given.shape, jnp.float32), fac, given, scratch=scratch)


def each(count, step):
    if count <= 8:
        for d in range(count):
            step(d)
    else:

        @pl.loop(0, count)
        def _(d):
            step(d)


def place_hot(places, cap, d):
    shape = (cap, places.shape[1])
    at = lax.broadcasted_iota(jnp.int32, shape, 0) + d * cap
    return (at == jnp.broadcast_to(places, shape)).astype(jnp.float32)


def line_hot(row, line_dev):
    shape = (line_dev, row.shape[1])
    at = lax.broadcasted_iota(jnp.int32, shape, 0)
    return (at == jnp.broadcast_to(row, shape)).astype(jnp.float32)


def pack_first_kernel(cap, rhs, owner_row, owner_col, within, places_out, out):
    slots = rhs.shape[1]
    shape = (slots, slots)
    row = jnp.broadcast_to(owner_row[...], shape)
    same = row == jnp.broadcast_to(owner_col[...], shape)
    before = lax.broadcasted_iota(jnp.int32, shape, 0) < lax.broadcasted_iota(jnp.int32, shape, 1)
    rank = jnp.sum((same & before).astype(jnp.float32), axis=0, keepdims=True).astype(jnp.int32)
    places = owner_row[...] * cap + rank
    places_out[...] = places
    tags = jnp.broadcast_to((within[...] + 1).astype(jnp.float32), (8, slots))
    full = jnp.concatenate([rhs[...], tags], axis=0)

    def step(d):
        out[d] = dot(full, place_hot(places_out[...], cap, d), NT)

    each(out.shape[0], step)


def pack_second_kernel(cap, rhs, lateral, first, low, high, places, out):
    rows, slots = rhs.shape
    lane = lax.broadcasted_iota(jnp.int32, (rows, slots), 1)
    here = first[...]
    below = jnp.where(lane == 0, jnp.broadcast_to(low[...], here.shape), pltpu.roll(here, 1, 1))
    above = jnp.where(
        lane == slots - 1, jnp.broadcast_to(high[...], here.shape), pltpu.roll(here, slots - 1, 1)
    )
    residual = rhs[...] + lateral[...] * (below + above)

    def step(d):
        out[d] = dot(residual, place_hot(places[...], cap, d), NT)

    each(out.shape[0], step)


def arrive_kernel(received, arrived, out, acc):
    acc[...] = jnp.zeros_like(acc)
    rows, line_dev = acc.shape

    def step(d):
        acc[...] += dot(received[d, :rows, :], line_hot(arrived[d], line_dev), NT)

    each(received.shape[0], step)
    quarter = out.shape[2]
    for q in range(out.shape[0]):
        out[q] = acc[:, q * quarter : (q + 1) * quarter]


def reply_kernel(returned, arrived, out):
    lines = jnp.concatenate([returned[q] for q in range(returned.shape[0])], axis=1)

    def step(d):
        out[d] = dot(lines, line_hot(arrived[d], lines.shape[1]), NN)

    each(out.shape[0], step)


def home_kernel(home, places, out):
    out[...] = jnp.zeros_like(out)
    cap = home.shape[2]

    def step(d):
        out[...] += dot(home[d], place_hot(places[...], cap, d), NN)

    each(home.shape[0], step)


def exchange(buffer, axis):
    return lax.all_to_all(buffer, axis, split_axis=0, concat_axis=0, tiled=True)


def body(rhs, lateral, piece_line, lower, diag_blocks, upper):
    fields, piece, line_dev = rhs.shape
    n_dom, n_sub = lax.axis_size("dom"), lax.axis_size("sub")
    mean_load = line_dev // n_dom
    cap = mean_load + (mean_load + 1) // 2
    rows = fields * piece
    f32 = lambda *shape: jax.ShapeDtypeStruct(shape, jnp.float32)
    rhs = rhs.reshape(rows, line_dev)
    lateral = lateral.reshape(rows, line_dev)
    owners = piece_line // line_dev
    within = piece_line % line_dev
    places, buffer = call(
        functools.partial(pack_first_kernel, cap),
        [jax.ShapeDtypeStruct((1, line_dev), jnp.int32), f32(n_dom, rows + 8, cap)],
        rhs, owners, owners.reshape(line_dev, 1), within,
    )
    received = exchange(buffer, "dom")
    fac = factor(lower, diag_blocks, upper)
    arrived = received[:, rows : rows + 1, :].astype(jnp.int32) - 1

    def finish(received):
        quarters = call(
            arrive_kernel, f32(n_sub, rows, line_dev // n_sub), received, arrived,
            scratch=[pltpu.VMEM((rows, line_dev), jnp.float32)],
        )
        solved = solve(fac, exchange(quarters, "sub"))
        reply = call(reply_kernel, f32(n_dom, rows, cap), exchange(solved, "sub"), arrived)
        return call(home_kernel, f32(rows, line_dev), exchange(reply, "dom"), places)

    first = finish(received)
    forward = [(i, i + 1) for i in range(n_dom - 1)]
    backward = [(b, a) for a, b in forward]
    low = lax.ppermute(first[:, line_dev - 1 :], "dom", forward)
    high = lax.ppermute(first[:, :1], "dom", backward)
    second = call(
        functools.partial(pack_second_kernel, cap), f32(n_dom, rows, cap),
        rhs, lateral, first, low, high, places,
    )
    return finish(exchange(second, "dom")).reshape(fields, piece, line_dev)


def solution(mesh):
    placed = (
        P(None, "sub", "dom"),
        P(None, "sub", "dom"),
        P("sub", "dom"),
        P(None, None, None, ("dom", "sub")),
        P(None, None, None, ("dom", "sub")),
        P(None, None, None, ("dom", "sub")),
    )
    return jax.shard_map(
        body, mesh=mesh, in_specs=placed, out_specs=P(None, "sub", "dom"), check_vma=False
    )
```

profile of v0, /device:TPU:0, one launch (start us, length us, event | category | flops | bytes accessed | tf_op | source)
XLA Modules:
  0.0 122.0 jit_solution(640524907284263100)
XLA Ops:
  2.5 1.7 %shard_map.65 = (s32[1,512]{1,0:T(1,128)S(1)}, f32[8,88,96]{2,1,0:T(8,128)S(1)}) custom-call(f32[80,512]{1,0:T(8,128)S(1)} %bitcast.4, s32[1,512]{1,0:T(1,128)S(1)} %and_select_fusion.1.owner_row, s32[512,1]{1,0:T(8,128)S(1)} %copy.7.owner_col, s32[1,512]{1,0:T(1,128)S(1)} %get-tuple-element.9.within), custom_call_target="tpu_custom_call" | custom-call | tf_op jit(solution)/shard_map/pallas_call | solution.py:24
  4.2 18.6 %all_to_all.40.received = f32[8,88,96]{2,1,0:T(8,128)S(1)} all-to-all(f32[8,88,96]{2,1,0:T(8,128)S(1)} %get-tuple-element.7), channel_id=1, replica_groups=mesh['dom'=8,'sub'=4] {'dom'}, dimensions={0} | all-to-all | bytes 540672 | tf_op jit(solution)/shard_map/all_to_all | solution.py:335
  22.8 2.9 %shard_map.66 = f32[4,80,128]{2,1,0:T(8,128)} custom-call(f32[8,88,96]{2,1,0:T(8,128)S(1)} %all_to_all.40.received, s32[8,1,96]{2,1,0:T(1,128)S(1)} %fusion.arrived), custom_call_target="tpu_custom_call" | custom-call | tf_op jit(solution)/shard_map/pallas_call | solution.py:24
  25.7 3.3 %all-to-all-start.1 = ((f32[4,80,128]{2,1,0:T(8,128)}), f32[4,80,128]{2,1,0:T(8,128)S(1)}, u32[]{:S(2)}, u32[]{:S(2)}) async-start(f32[4,80,128]{2,1,0:T(8,128)} %shard_map.66), calls=%async_computation.1 | async-start | bytes 327680 | tf_op jit(solution)/shard_map/all_to_all | solution.py:335
  30.2 1.1 copy-done.4
  31.3 1.1 copy-done.5
  32.5 2.7 %shard_map.64.fac = f32[5,5,336,128]{3,2,1,0:T(8,128)S(1)} custom-call(f32[5,5,64,128]{3,2,1,0:T(8,128)S(1)} %copy-done.3, f32[5,5,64,128]{3,2,1,0:T(8,128)S(1)} %copy-done.4, f32[5,5,64,128]{3,2,1,0:T(8,128)S(1)} %copy-done.5), custom_call_target="tpu_custom_call" | custom-call | tf_op jit(solution)/shard_map/pallas_call | solution.py:24
  35.2 2.0 %copy-done = f32[5,5,336,128]{3,2,1,0:T(8,128)} copy-done((f32[5,5,336,128]{3,2,1,0:T(8,128)}, f32[5,5,336,128]{3,2,1,0:T(8,128)S(1)}, u32[]{:S(2)}) %copy-start) | copy-done | bytes 4300824
  37.1 2.2 %copy-done.1 = f32[5,5,336,128]{3,2,1,0:T(8,128)S(1)} copy-done((f32[5,5,336,128]{3,2,1,0:T(8,128)S(1)}, f32[5,5,336,128]{3,2,1,0:T(8,128)}, u32[]{:S(2)}) %copy-start.1) | copy-done | bytes 4300824
  39.7 8.3 %all_to_all.41.returned = f32[4,80,128]{2,1,0:T(8,128)S(1)} all-to-all(f32[4,80,128]{2,1,0:T(8,128)S(1)} %shard_map.67), channel_id=1, replica_groups=mesh['dom'=8,'sub'=4] {'sub'}, dimensions={0} | all-to-all | bytes 327680 | tf_op jit(solution)/shard_map/all_to_all | solution.py:335
  48.0 1.4 %shard_map.68 = f32[8,80,96]{2,1,0:T(8,128)S(1)} custom-call(f32[4,80,128]{2,1,0:T(8,128)S(1)} %all_to_all.41.returned, s32[8,1,96]{2,1,0:T(1,128)S(1)} %fusion.arrived), custom_call_target="tpu_custom_call" | custom-call | tf_op jit(solution)/shard_map/pallas_call | solution.py:24
  49.4 13.9 %all_to_all.42.home = f32[8,80,96]{2,1,0:T(8,128)S(1)} all-to-all(f32[8,80,96]{2,1,0:T(8,128)S(1)} %shard_map.68), channel_id=1, replica_groups=mesh['dom'=8,'sub'=4] {'dom'}, dimensions={0} | all-to-all | bytes 491520 | tf_op jit(solution)/shard_map/all_to_all | solution.py:335
  63.3 1.3 %shard_map.69.first = f32[80,512]{1,0:T(8,128)S(1)} custom-call(f32[8,80,96]{2,1,0:T(8,128)S(1)} %all_to_all.42.home, s32[1,512]{1,0:T(1,128)S(1)} %get-tuple-element.8.places), custom_call_target="tpu_custom_call" | custom-call | tf_op jit(solution)/shard_map/pallas_call | solution.py:24
  64.7 1.3 %collective-permute-start.1 = (f32[80,1]{1,0:T(8,128)S(1)}, f32[80,1]{1,0:T(8,128)S(1)}, u32[]{:S(2)}, u32[]{:S(2)}) collective-permute-start(f32[80,1]{1,0:T(8,128)S(1)} %get-tuple-element.11), channel_id=1, source_target_pairs={{4,0},{8,4},{12,8},{16,12},{20,16},{24,20},{28,24},{5,1},{9,5},{13... | collective-permute-start | bytes 968 | tf_op jit(solution)/shard_map/ppermute | solution.py:371
  65.9 4.5 %collective-permute-start = (f32[80,1]{1,0:T(8,128)S(1)}, f32[80,1]{1,0:T(8,128)S(1)}, u32[]{:S(2)}, u32[]{:S(2)}) collective-permute-start(f32[80,1]{1,0:T(8,128)S(1)} %get-tuple-element.12), channel_id=1, source_target_pairs={{0,4},{4,8},{8,12},{12,16},{16,20},{20,24},{24,28},{1,5},{5,9},{9,... | collective-permute-start | bytes 968 | tf_op jit(solution)/shard_map/ppermute | solution.py:370
  70.5 1.6 %collective-permute-done.low = f32[80,1]{1,0:T(8,128)S(1)} collective-permute-done((f32[80,1]{1,0:T(8,128)S(1)}, f32[80,1]{1,0:T(8,128)S(1)}, u32[]{:S(2)}, u32[]{:S(2)}) %collective-permute-start) | collective-permute-done | bytes 352 | tf_op jit(solution)/shard_map/ppermute | solution.py:370
  72.2 1.8 %shard_map.70 = f32[8,80,96]{2,1,0:T(8,128)S(1)} custom-call(f32[80,512]{1,0:T(8,128)S(1)} %bitcast.5, f32[80,512]{1,0:T(8,128)S(1)} %bitcast.6, f32[80,512]{1,0:T(8,128)S(1)} %shard_map.69.first, f32[80,1]{1,0:T(8,128)S(1)} %collective-permute-done.low, f32[80,1]{1,0:T(8,128)S(1)} %collective-permute-done.1.high, s32[1,512]{1,0:T(1,128)S(1)} %get-tuple-element.8.places), custom_call_target="tpu_custom_call" | custom-call | tf_op jit(solution)/shard_map/pallas_call | solution.py:24
  74.0 13.6 %all_to_all.43.received = f32[8,80,96]{2,1,0:T(8,128)S(1)} all-to-all(f32[8,80,96]{2,1,0:T(8,128)S(1)} %shard_map.70), channel_id=1, replica_groups=mesh['dom'=8,'sub'=4] {'dom'}, dimensions={0} | all-to-all | bytes 491520 | tf_op jit(solution)/shard_map/all_to_all | solution.py:335
  87.6 2.3 %shard_map.71 = f32[4,80,128]{2,1,0:T(8,128)S(1)} custom-call(f32[8,80,96]{2,1,0:T(8,128)S(1)} %all_to_all.43.received, s32[8,1,96]{2,1,0:T(1,128)S(1)} %fusion.arrived), custom_call_target="tpu_custom_call" | custom-call | tf_op jit(solution)/shard_map/pallas_call | solution.py:24
  89.9 7.3 %all_to_all.44.given = f32[4,80,128]{2,1,0:T(8,128)S(1)} all-to-all(f32[4,80,128]{2,1,0:T(8,128)S(1)} %shard_map.71), channel_id=1, replica_groups=mesh['dom'=8,'sub'=4] {'sub'}, dimensions={0} | all-to-all | bytes 327680 | tf_op jit(solution)/shard_map/all_to_all | solution.py:335
  97.6 7.3 %all_to_all.45.returned = f32[4,80,128]{2,1,0:T(8,128)S(1)} all-to-all(f32[4,80,128]{2,1,0:T(8,128)S(1)} %shard_map.72), channel_id=1, replica_groups=mesh['dom'=8,'sub'=4] {'sub'}, dimensions={0} | all-to-all | bytes 327680 | tf_op jit(solution)/shard_map/all_to_all | solution.py:335
  105.0 1.4 %shard_map.73 = f32[8,80,96]{2,1,0:T(8,128)S(1)} custom-call(f32[4,80,128]{2,1,0:T(8,128)S(1)} %all_to_all.45.returned, s32[8,1,96]{2,1,0:T(1,128)S(1)} %fusion.arrived), custom_call_target="tpu_custom_call" | custom-call | tf_op jit(solution)/shard_map/pallas_call | solution.py:24
  106.3 13.8 %all_to_all.46.home = f32[8,80,96]{2,1,0:T(8,128)S(1)} all-to-all(f32[8,80,96]{2,1,0:T(8,128)S(1)} %shard_map.73), channel_id=1, replica_groups=mesh['dom'=8,'sub'=4] {'dom'}, dimensions={0} | all-to-all | bytes 491520 | tf_op jit(solution)/shard_map/all_to_all | solution.py:335
  120.1 1.9 %shard_map.74 = f32[80,512]{1,0:T(8,128)} custom-call(f32[8,80,96]{2,1,0:T(8,128)S(1)} %all_to_all.46.home, s32[1,512]{1,0:T(1,128)S(1)} %get-tuple-element.8.places), custom_call_target="tpu_custom_call" | custom-call | tf_op jit(solution)/shard_map/pallas_call | solution.py:24
  (23 shorter events, 4.5 us)
Async XLA Ops:
  1.5 0.9 copy-start.6
  25.7 11.5 %all-to-all-start.1 = ((f32[4,80,128]{2,1,0:T(8,128)}), f32[4,80,128]{2,1,0:T(8,128)S(1)}, u32[]{:S(2)}, u32[]{:S(2)}) async-start(f32[4,80,128]{2,1,0:T(8,128)} %shard_map.66), calls=%async_computation.1 | async-start | bytes 327680 | tf_op jit(solution)/shard_map/all_to_all | solution.py:335
  29.0 1.1 copy-start.3
  30.2 1.1 copy-start.4
  31.3 1.1 copy-start.5
  35.2 2.0 %copy-start = (f32[5,5,336,128]{3,2,1,0:T(8,128)}, f32[5,5,336,128]{3,2,1,0:T(8,128)S(1)}, u32[]{:S(2)}) copy-start(f32[5,5,336,128]{3,2,1,0:T(8,128)S(1)} %shard_map.64.fac) | copy-start | bytes 12902404
  37.1 2.2 %copy-start.1 = (f32[5,5,336,128]{3,2,1,0:T(8,128)S(1)}, f32[5,5,336,128]{3,2,1,0:T(8,128)}, u32[]{:S(2)}) copy-start(f32[5,5,336,128]{3,2,1,0:T(8,128)} %copy-done) | copy-start | bytes 12902404
  39.4 32.8 %copy-start.7 = (f32[5,16,512]{2,1,0:T(8,128)S(1)}, f32[5,16,512]{2,1,0:T(8,128)}, u32[]{:S(2)}) copy-start(f32[5,16,512]{2,1,0:T(8,128)} %param.6) | copy-start | bytes 491524
  39.4 32.8 %copy-start.8 = (f32[5,16,512]{2,1,0:T(8,128)S(1)}, f32[5,16,512]{2,1,0:T(8,128)}, u32[]{:S(2)}) copy-start(f32[5,16,512]{2,1,0:T(8,128)} %param.7) | copy-start | bytes 491524
  39.4 57.8 %copy-start.2 = (f32[5,5,336,128]{3,2,1,0:T(8,128)S(1)}, f32[5,5,336,128]{3,2,1,0:T(8,128)}, u32[]{:S(2)}) copy-start(f32[5,5,336,128]{3,2,1,0:T(8,128)} %copy-done) | copy-start | bytes 12902404
  64.7 5.9 %collective-permute-start.1 = (f32[80,1]{1,0:T(8,128)S(1)}, f32[80,1]{1,0:T(8,128)S(1)}, u32[]{:S(2)}, u32[]{:S(2)}) collective-permute-start(f32[80,1]{1,0:T(8,128)S(1)} %get-tuple-element.11), channel_id=1, source_target_pairs={{4,0},{8,4},{12,8},{16,12},{20,16},{24,20},{28,24},{5,1},{9,5},{13... | collective-permute-start | bytes 968 | tf_op jit(solution)/shard_map/ppermute | solution.py:371
  65.9 6.2 %collective-permute-start = (f32[80,1]{1,0:T(8,128)S(1)}, f32[80,1]{1,0:T(8,128)S(1)}, u32[]{:S(2)}, u32[]{:S(2)}) collective-permute-start(f32[80,1]{1,0:T(8,128)S(1)} %get-tuple-element.12), channel_id=1, source_target_pairs={{0,4},{4,8},{8,12},{12,16},{16,20},{20,24},{24,28},{1,5},{5,9},{9,... | collective-permute-start | bytes 968 | tf_op jit(solution)/shard_map/ppermute | solution.py:370
where the time goes:
time: 123 us; the launch traced here: 122 us
  blocking collectives  82.9 us (67%)
  Pallas kernels  18 us (15%)
  starting transfers between devices  9.18 us (7%)
  local copies, waits for them, and re-layouts  8.76 us (7%)
  waiting for transfers between devices  1.66 us (1%)
  other arithmetic  1.39 us (1%)
    all_to_all x7, blocking collectives, exchange(): return lax.all_to_all(buffer, axis, split_axis=0, concat_axis=0, tiled=True)  82.9 us
    pallas_call x11, Pallas kernels, call(): pl.pallas_call(kernel, out_shape=outs, in_specs=[VMEM] * len(args), out_s...  18 us
    unnamed x18, local copies, waits for them, and re-layouts  8.54 us
    ppermute x1, starting transfers between devices, body(): low = lax.ppermute(first[:, line_dev - 1:], 'dom', forward)  4.55 us
    all_to_all x1, starting transfers between devices, exchange(): return lax.all_to_all(buffer, axis, split_axis=0, concat_axis=0, tiled=True)  3.35 us
  transfers between devices with their start and end apart: 3, of which 1 were waited for; matrix products, arithmetic and copies ran while one was open for 0% of the time, Pallas kernels for 2%

commit v1 on v0

--- a/solution.py
+++ b/solution.py
@@ -12,6 +12,7 @@
 PARAMS = pltpu.CompilerParams(vmem_limit_bytes=40 * 1024 * 1024)
 NT = (((1,), (1,)), ((), ()))
 NN = (((1,), (0,)), ((), ()))
+MESH = pl.DeviceIdType.MESH
 
 
 def dot(left, right, dims):
@@ -20,14 +21,14 @@
     )
 
 
-def call(kernel, outs, *args, scratch=()):
+def call(kernel, outs, *args, scratch=(), params=PARAMS):
     return pl.pallas_call(
         kernel,
         out_shape=outs,
         in_specs=[VMEM] * len(args),
         out_specs=jax.tree.map(lambda _: VMEM, outs),
         scratch_shapes=list(scratch),
-        compiler_params=PARAMS,
+        compiler_params=params,
     )(*args)
 
 
@@ -283,13 +284,32 @@
     each(out.shape[0], step)
 
 
-def pack_second_kernel(cap, rhs, lateral, first, low, high, places, out):
+def pack_second_kernel(cap, rhs, lateral, first, places, out, low_edge, high_edge, send, recv):
     rows, slots = rhs.shape
+    count = lax.axis_size("dom")
+    me = lax.axis_index("dom")
+    right, left = lax.rem(me + 1, count), lax.rem(me + count - 1, count)
+    greet("dom", [right, left])
+    copies = [
+        pltpu.make_async_remote_copy(
+            src_ref=first.at[:, pl.ds(start, 128)], dst_ref=edge, send_sem=send.at[i],
+            recv_sem=recv.at[i], device_id={"dom": other}, device_id_type=MESH,
+        )
+        for i, (start, edge, other) in enumerate(
+            ((slots - 128, low_edge, right), (0, high_edge, left))
+        )
+    ]
+    for copy in copies:
+        copy.start()
+    for copy in copies:
+        copy.wait()
+    low = jnp.where(me == 0, 0.0, low_edge[:, 127:128])
+    high = jnp.where(me == count - 1, 0.0, high_edge[:, 0:1])
     lane = lax.broadcasted_iota(jnp.int32, (rows, slots), 1)
     here = first[...]
-    below = jnp.where(lane == 0, jnp.broadcast_to(low[...], here.shape), pltpu.roll(here, 1, 1))
+    below = jnp.where(lane == 0, jnp.broadcast_to(low, here.shape), pltpu.roll(here, 1, 1))
     above = jnp.where(
-        lane == slots - 1, jnp.broadcast_to(high[...], here.shape), pltpu.roll(here, slots - 1, 1)
+        lane == slots - 1, jnp.broadcast_to(high, here.shape), pltpu.roll(here, slots - 1, 1)
     )
     residual = rhs[...] + lateral[...] * (below + above)
 
@@ -331,8 +351,52 @@
     each(home.shape[0], step)
 
 
-def exchange(buffer, axis):
-    return lax.all_to_all(buffer, axis, split_axis=0, concat_axis=0, tiled=True)
+def greet(axis, others):
+    barrier = pltpu.get_barrier_semaphore()
+    for other in others:
+        pl.semaphore_signal(barrier, inc=1, device_id={axis: other}, device_id_type=MESH)
+    pl.semaphore_wait(barrier, len(others))
+
+
+def exchange_kernel(axis, given, out, send, recv, own):
+    count = given.shape[0]
+    me = lax.axis_index(axis)
+    keep = pltpu.make_async_copy(given.at[me], out.at[me], own)
+    keep.start()
+    greet(axis, [lax.rem(me + i, count) for i in range(1, count)])
+
+    def copy(i, source, target, other):
+        return pltpu.make_async_remote_copy(
+            src_ref=given.at[source], dst_ref=out.at[target], send_sem=send.at[i],
+            recv_sem=recv.at[i], device_id={axis: other}, device_id_type=MESH,
+        )
+
+    for i in range(1, count):
+        other = lax.rem(me + i, count)
+        copy(i, other, me, other).start()
+    for i in range(1, count):
+        other = lax.rem(me + count - i, count)
+        copy(i, other, other, other).wait_recv()
+    for i in range(1, count):
+        other = lax.rem(me + i, count)
+        copy(i, other, me, other).wait_send()
+    keep.wait()
+
+
+def exchange(buffer, axis, number):
+    count = buffer.shape[0]
+    return pl.pallas_call(
+        functools.partial(exchange_kernel, axis),
+        out_shape=jax.ShapeDtypeStruct(buffer.shape, buffer.dtype),
+        in_specs=[VMEM],
+        out_specs=VMEM,
+        scratch_shapes=[
+            pltpu.SemaphoreType.DMA((count,)), pltpu.SemaphoreType.DMA((count,)), pltpu.SemaphoreType.DMA,
+        ],
+        compiler_params=pltpu.CompilerParams(
+            vmem_limit_bytes=40 * 1024 * 1024, collective_id=number, has_side_effects=True
+        ),
+    )(buffer)
 
 
 def body(rhs, lateral, piece_line, lower, diag_blocks, upper):
@@ -351,7 +415,7 @@
         [jax.ShapeDtypeStruct((1, line_dev), jnp.int32), f32(n_dom, rows + 8, cap)],
         rhs, owners, owners.reshape(line_dev, 1), within,
     )
-    received = exchange(buffer, "dom")
+    received = exchange(buffer, "dom", 0)
     fac = factor(lower, diag_blocks, upper)
     arrived = received[:, rows : rows + 1, :].astype(jnp.int32) - 1
 
@@ -360,20 +424,20 @@
             arrive_kernel, f32(n_sub, rows, line_dev // n_sub), received, arrived,
             scratch=[pltpu.VMEM((rows, line_dev), jnp.float32)],
         )
-        solved = solve(fac, exchange(quarters, "sub"))
-        reply = call(reply_kernel, f32(n_dom, rows, cap), exchange(solved, "sub"), arrived)
-        return call(home_kernel, f32(rows, line_dev), exchange(reply, "dom"), places)
+        solved = solve(fac, exchange(quarters, "sub", 2))
+        reply = call(reply_kernel, f32(n_dom, rows, cap), exchange(solved, "sub", 2), arrived)
+        return call(home_kernel, f32(rows, line_dev), exchange(reply, "dom", 1), places)
 
     first = finish(received)
-    forward = [(i, i + 1) for i in range(n_dom - 1)]
-    backward = [(b, a) for a, b in forward]
-    low = lax.ppermute(first[:, line_dev - 1 :], "dom", forward)
-    high = lax.ppermute(first[:, :1], "dom", backward)
     second = call(
         functools.partial(pack_second_kernel, cap), f32(n_dom, rows, cap),
-        rhs, lateral, first, low, high, places,
-    )
-    return finish(exchange(second, "dom")).reshape(fields, piece, line_dev)
+        rhs, lateral, first, places,
+        scratch=[pltpu.VMEM((rows, 128), jnp.float32)] * 2 + [pltpu.SemaphoreType.DMA((2,))] * 2,
+        params=pltpu.CompilerParams(
+            vmem_limit_bytes=40 * 1024 * 1024, collective_id=3, has_side_effects=True
+        ),
+    )
+    return finish(exchange(second, "dom", 1)).reshape(fields, piece, line_dev)
 
 
 def solution(mesh):

time: 123 us -> 95.1 us (0.77)
  blocking collectives: 82.9 us -> 0 us
  Pallas kernels: 18 us -> 88.7 us
  starting transfers between devices: 9.18 us -> 0 us
  local copies, waits for them, and re-layouts: 8.76 us -> 4.5 us
  waiting for transfers between devices: 1.66 us -> 0 us
    all_to_all x7 -> x0, blocking collectives: 82.9 us -> none  [exchange(): return lax.all_to_all(buffer, axis, split_axis=0, concat_axis=0, tiled=True)]
    pallas_call x0 -> x8, Pallas kernels: none -> 63.3 us  [exchange(): pl.pallas_call(functools.partial(exchange_kernel, axis), out_shape=jax.Sh...]
    pallas_call x11, Pallas kernels: 18 us -> 25.3 us  [call(): pl.pallas_call(kernel, out_shape=outs, in_specs=[VMEM] * len(args), out_s...]
    ppermute x2 -> x0, starting transfers between devices: 5.83 us -> none  [the longest x1 4.55 us: body(): low = lax.ppermute(first[:, line_dev - 1:], 'dom', forward)]
    unnamed x18 -> x12, local copies, waits for them, and re-layouts: 8.54 us -> 4.36 us
    all_to_all x1 -> x0, starting transfers between devices: 3.35 us -> none  [exchange(): return lax.all_to_all(buffer, axis, split_axis=0, concat_axis=0, tiled=True)]
    ppermute x2 -> x0, waiting for transfers between devices: 1.65 us -> none  [the longest x1 1.61 us: body(): low = lax.ppermute(first[:, line_dev - 1:], 'dom', forward)]
  transfers between devices with their start and end apart: 3 -> 0, of which waited for: 1 -> 0; matrix products, arithmetic and copies ran while one was open for 0% -> 0% of each run, Pallas kernels for 2% -> 0%
where the time goes in v1:
time: 95.1 us; the launch traced here: 94.7 us
  Pallas kernels  88.7 us (93%)
  local copies, waits for them, and re-layouts  4.5 us (5%)
  other arithmetic  1.39 us (1%)
    pallas_call x8, Pallas kernels, exchange(): pl.pallas_call(functools.partial(exchange_kernel, axis), out_shape=jax.Sh...  63.3 us
    pallas_call x11, Pallas kernels, call(): pl.pallas_call(kernel, out_shape=outs, in_specs=[VMEM] * len(args), out_s...  25.3 us
    unnamed x12, local copies, waits for them, and re-layouts  4.36 us

profile of v1, /device:TPU:0, one launch (start us, length us, event | category | flops | bytes accessed | tf_op | source)
XLA Modules:
  0.0 94.7 jit_solution(14290865061414852107)
XLA Ops:
  0.0 0.7 and_select_fusion
  0.7 0.7 and_select_fusion.1.owner_row
  1.6 0.9 copy-done.3
  2.5 1.7 %shard_map.65 = (s32[1,512]{1,0:T(1,128)S(1)}, f32[8,88,96]{2,1,0:T(8,128)S(1)}) custom-call(f32[80,512]{1,0:T(8,128)S(1)} %bitcast.4, s32[1,512]{1,0:T(1,128)S(1)} %and_select_fusion.1.owner_row, s32[512,1]{1,0:T(8,128)S(1)} %copy.7.owner_col, s32[1,512]{1,0:T(1,128)S(1)} %get-tuple-element.9.within), custom_call_target="tpu_custom_call" | custom-call | tf_op jit(solution)/shard_map/pallas_call | solution.py:25
  4.2 12.2 %shard_map.66.received = f32[8,88,96]{2,1,0:T(8,128)S(1)} custom-call(f32[8,88,96]{2,1,0:T(8,128)S(1)} %get-tuple-element.7.given), custom_call_target="tpu_custom_call" | custom-call | tf_op jit(solution)/shard_map/pallas_call | solution.py:388
  16.4 2.3 %shard_map.67.given = f32[4,80,128]{2,1,0:T(8,128)S(1)} custom-call(f32[8,88,96]{2,1,0:T(8,128)S(1)} %shard_map.66.received, s32[8,1,96]{2,1,0:T(1,128)S(1)} %convert_add_fusion.arrived), custom_call_target="tpu_custom_call" | custom-call | tf_op jit(solution)/shard_map/pallas_call | solution.py:25
  18.7 4.5 %shard_map.68.given = f32[4,80,128]{2,1,0:T(8,128)S(1)} custom-call(f32[4,80,128]{2,1,0:T(8,128)S(1)} %shard_map.67.given), custom_call_target="tpu_custom_call" | custom-call | tf_op jit(solution)/shard_map/pallas_call | solution.py:388
  23.2 1.1 %copy-done = f32[5,5,64,128]{3,2,1,0:T(8,128)S(1)} copy-done((f32[5,5,64,128]{3,2,1,0:T(8,128)S(1)}, f32[5,5,64,128]{3,2,1,0:T(8,128)}, u32[]{:S(2)}) %copy-start) | copy-done | bytes 819224
  24.3 1.1 %copy-done.1 = f32[5,5,64,128]{3,2,1,0:T(8,128)S(1)} copy-done((f32[5,5,64,128]{3,2,1,0:T(8,128)S(1)}, f32[5,5,64,128]{3,2,1,0:T(8,128)}, u32[]{:S(2)}) %copy-start.1) | copy-done | bytes 819224
  25.5 1.1 %copy-done.2 = f32[5,5,64,128]{3,2,1,0:T(8,128)S(1)} copy-done((f32[5,5,64,128]{3,2,1,0:T(8,128)S(1)}, f32[5,5,64,128]{3,2,1,0:T(8,128)}, u32[]{:S(2)}) %copy-start.2) | copy-done | bytes 819224
  26.6 2.7 %shard_map.64.fac = f32[5,5,336,128]{3,2,1,0:T(8,128)S(1)} custom-call(f32[5,5,64,128]{3,2,1,0:T(8,128)S(1)} %copy-done, f32[5,5,64,128]{3,2,1,0:T(8,128)S(1)} %copy-done.1, f32[5,5,64,128]{3,2,1,0:T(8,128)S(1)} %copy-done.2), custom_call_target="tpu_custom_call" | custom-call | tf_op jit(solution)/shard_map/pallas_call | solution.py:25
  29.4 0.4 shard_map.69.given
  29.8 4.5 %shard_map.70.returned = f32[4,80,128]{2,1,0:T(8,128)S(1)} custom-call(f32[4,80,128]{2,1,0:T(8,128)S(1)} %shard_map.69.given), custom_call_target="tpu_custom_call" | custom-call | tf_op jit(solution)/shard_map/pallas_call | solution.py:388
  34.3 1.4 %shard_map.71.given = f32[8,80,96]{2,1,0:T(8,128)S(1)} custom-call(f32[4,80,128]{2,1,0:T(8,128)S(1)} %shard_map.70.returned, s32[8,1,96]{2,1,0:T(1,128)S(1)} %convert_add_fusion.arrived), custom_call_target="tpu_custom_call" | custom-call | tf_op jit(solution)/shard_map/pallas_call | solution.py:25
  35.7 12.2 %shard_map.72.home = f32[8,80,96]{2,1,0:T(8,128)S(1)} custom-call(f32[8,80,96]{2,1,0:T(8,128)S(1)} %shard_map.71.given), custom_call_target="tpu_custom_call" | custom-call | tf_op jit(solution)/shard_map/pallas_call | solution.py:388
  47.9 1.3 %shard_map.73.first = f32[80,512]{1,0:T(8,128)S(1)} custom-call(f32[8,80,96]{2,1,0:T(8,128)S(1)} %shard_map.72.home, s32[1,512]{1,0:T(1,128)S(1)} %get-tuple-element.8.places), custom_call_target="tpu_custom_call" | custom-call | tf_op jit(solution)/shard_map/pallas_call | solution.py:25
  49.2 9.7 %shard_map.74.given = f32[8,80,96]{2,1,0:T(8,128)S(1)} custom-call(f32[80,512]{1,0:T(8,128)S(1)} %bitcast.5, f32[80,512]{1,0:T(8,128)S(1)} %bitcast.6, f32[80,512]{1,0:T(8,128)S(1)} %shard_map.73.first, s32[1,512]{1,0:T(1,128)S(1)} %get-tuple-element.8.places), custom_call_target="tpu_custom_call" | custom-call | tf_op jit(solution)/shard_map/pallas_call | solution.py:25
  58.9 9.7 %shard_map.75.received = f32[8,80,96]{2,1,0:T(8,128)S(1)} custom-call(f32[8,80,96]{2,1,0:T(8,128)S(1)} %shard_map.74.given), custom_call_target="tpu_custom_call" | custom-call | tf_op jit(solution)/shard_map/pallas_call | solution.py:388
  68.6 2.3 %shard_map.76.given = f32[4,80,128]{2,1,0:T(8,128)S(1)} custom-call(f32[8,80,96]{2,1,0:T(8,128)S(1)} %shard_map.75.received, s32[8,1,96]{2,1,0:T(1,128)S(1)} %convert_add_fusion.arrived), custom_call_target="tpu_custom_call" | custom-call | tf_op jit(solution)/shard_map/pallas_call | solution.py:25
  70.8 4.5 %shard_map.77.given = f32[4,80,128]{2,1,0:T(8,128)S(1)} custom-call(f32[4,80,128]{2,1,0:T(8,128)S(1)} %shard_map.76.given), custom_call_target="tpu_custom_call" | custom-call | tf_op jit(solution)/shard_map/pallas_call | solution.py:388
  75.8 4.7 %shard_map.79.returned = f32[4,80,128]{2,1,0:T(8,128)S(1)} custom-call(f32[4,80,128]{2,1,0:T(8,128)S(1)} %shard_map.78.given), custom_call_target="tpu_custom_call" | custom-call | tf_op jit(solution)/shard_map/pallas_call | solution.py:388
  80.4 1.4 %shard_map.80.given = f32[8,80,96]{2,1,0:T(8,128)S(1)} custom-call(f32[4,80,128]{2,1,0:T(8,128)S(1)} %shard_map.79.returned, s32[8,1,96]{2,1,0:T(1,128)S(1)} %convert_add_fusion.arrived), custom_call_target="tpu_custom_call" | custom-call | tf_op jit(solution)/shard_map/pallas_call | solution.py:25
  81.8 11.0 %shard_map.81.home = f32[8,80,96]{2,1,0:T(8,128)S(1)} custom-call(f32[8,80,96]{2,1,0:T(8,128)S(1)} %shard_map.80.given), custom_call_target="tpu_custom_call" | custom-call | tf_op jit(solution)/shard_map/pallas_call | solution.py:388
  92.8 1.9 %shard_map.82 = f32[80,512]{1,0:T(8,128)} custom-call(f32[8,80,96]{2,1,0:T(8,128)S(1)} %shard_map.81.home, s32[1,512]{1,0:T(1,128)S(1)} %get-tuple-element.8.places), custom_call_target="tpu_custom_call" | custom-call | tf_op jit(solution)/shard_map/pallas_call | solution.py:25
  (11 shorter events, 0.6 us)
Async XLA Ops:
  1.5 0.9 copy-start.3
  23.2 1.1 %copy-start = (f32[5,5,64,128]{3,2,1,0:T(8,128)S(1)}, f32[5,5,64,128]{3,2,1,0:T(8,128)}, u32[]{:S(2)}) copy-start(f32[5,5,64,128]{3,2,1,0:T(8,128)} %low.1) | copy-start | bytes 2457604
  24.3 1.1 %copy-start.1 = (f32[5,5,64,128]{3,2,1,0:T(8,128)S(1)}, f32[5,5,64,128]{3,2,1,0:T(8,128)}, u32[]{:S(2)}) copy-start(f32[5,5,64,128]{3,2,1,0:T(8,128)} %mid.1) | copy-start | bytes 2457604
  25.5 1.1 %copy-start.2 = (f32[5,5,64,128]{3,2,1,0:T(8,128)S(1)}, f32[5,5,64,128]{3,2,1,0:T(8,128)}, u32[]{:S(2)}) copy-start(f32[5,5,64,128]{3,2,1,0:T(8,128)} %high.1) | copy-start | bytes 2457604
  29.4 19.8 %copy-start.4 = (f32[5,16,512]{2,1,0:T(8,128)S(1)}, f32[5,16,512]{2,1,0:T(8,128)}, u32[]{:S(2)}) copy-start(f32[5,16,512]{2,1,0:T(8,128)} %param.6) | copy-start | bytes 491524
  29.4 19.8 %copy-start.5 = (f32[5,16,512]{2,1,0:T(8,128)S(1)}, f32[5,16,512]{2,1,0:T(8,128)}, u32[]{:S(2)}) copy-start(f32[5,16,512]{2,1,0:T(8,128)} %param.7) | copy-start | bytes 491524

commit v2 on v1

--- a/solution.py
+++ b/solution.py
@@ -21,11 +21,11 @@
     )
 
 
-def call(kernel, outs, *args, scratch=(), params=PARAMS):
+def call(kernel, outs, *args, scratch=(), params=PARAMS, space=VMEM):
     return pl.pallas_call(
         kernel,
         out_shape=outs,
-        in_specs=[VMEM] * len(args),
+        in_specs=[space] * len(args),
         out_specs=jax.tree.map(lambda _: VMEM, outs),
         scratch_shapes=list(scratch),
         compiler_params=params,
@@ -99,15 +99,22 @@
     sizes, base = levels_of(count)
     depth = len(sizes)
     lows, mids, highs = scratch[:depth], scratch[depth : 2 * depth], scratch[2 * depth : 3 * depth]
-    inv_buf, low_pad, inv_pad, high_pad = scratch[3 * depth :]
-    for source, target in ((low, lows[0]), (mid, mids[0]), (high, highs[0])):
-        target[:, :, :count, :] = source[...]
+    inv_buf, low_pad, inv_pad, high_pad, loaded = scratch[3 * depth :]
+    loads = [
+        pltpu.make_async_copy(source.at[i], target.at[i, :, pl.ds(0, count), :], loaded.at[n * F + i])
+        for n, (source, target) in enumerate(((low, lows[0]), (mid, mids[0]), (high, highs[0])))
+        for i in range(F)
+    ]
+    for copy in loads:
+        copy.start()
     for group in (lows, mids, highs):
         for buf in group:
             rows = buf.shape[2]
             buf[:, :, rows - 8 :, :] = jnp.zeros((F, F, 8, buf.shape[3]), jnp.float32)
     for buf in (low_pad, inv_pad, high_pad):
         buf[...] = jnp.zeros_like(buf)
+    for copy in loads:
+        copy.wait()
     last = None
     for level, (half, at) in enumerate(sizes):
         lo, mi, hi = lows[level], mids[level], highs[level]
@@ -157,9 +164,9 @@
     sizes, base = levels_of(count)
     pads = [pltpu.VMEM((F, F, 2 * half + 8, lanes), jnp.float32) for half, _ in sizes]
     scratch = pads * 3 + [pltpu.VMEM((F, F, count // 2 + 8, lanes), jnp.float32)]
-    scratch += [pltpu.VMEM((F, F, 24, lanes), jnp.float32)] * 3
+    scratch += [pltpu.VMEM((F, F, 24, lanes), jnp.float32)] * 3 + [pltpu.SemaphoreType.DMA((3 * F,))]
     out = jax.ShapeDtypeStruct((F, F, base + 56, lanes), jnp.float32)
-    return call(factor_kernel, out, low, mid, high, scratch=scratch)
+    return call(factor_kernel, out, low, mid, high, scratch=scratch, space=pl.BlockSpec(memory_space=pltpu.HBM))
 
 
 def vload(ref, rows):
@@ -243,15 +250,15 @@
     return call(solve_kernel, jax.ShapeDtypeStruct(given.shape, jnp.float32), fac, given, scratch=scratch)
 
 
-def each(count, step):
+def each(first, count, step):
     if count <= 8:
-        for d in range(count):
-            step(d)
+        for i in range(first, count):
+            step(i)
     else:
 
-        @pl.loop(0, count)
-        def _(d):
-            step(d)
+        @pl.loop(first, count)
+        def _(i):
+            step(i)
 
 
 def place_hot(places, cap, d):
@@ -264,91 +271,6 @@
     shape = (line_dev, row.shape[1])
     at = lax.broadcasted_iota(jnp.int32, shape, 0)
     return (at == jnp.broadcast_to(row, shape)).astype(jnp.float32)
-
-
-def pack_first_kernel(cap, rhs, owner_row, owner_col, within, places_out, out):
-    slots = rhs.shape[1]
-    shape = (slots, slots)
-    row = jnp.broadcast_to(owner_row[...], shape)
-    same = row == jnp.broadcast_to(owner_col[...], shape)
-    before = lax.broadcasted_iota(jnp.int32, shape, 0) < lax.broadcasted_iota(jnp.int32, shape, 1)
-    rank = jnp.sum((same & before).astype(jnp.float32), axis=0, keepdims=True).astype(jnp.int32)
-    places = owner_row[...] * cap + rank
-    places_out[...] = places
-    tags = jnp.broadcast_to((within[...] + 1).astype(jnp.float32), (8, slots))
-    full = jnp.concatenate([rhs[...], tags], axis=0)
-
-    def step(d):
-        out[d] = dot(full, place_hot(places_out[...], cap, d), NT)
-
-    each(out.shape[0], step)
-
-
-def pack_second_kernel(cap, rhs, lateral, first, places, out, low_edge, high_edge, send, recv):
-    rows, slots = rhs.shape
-    count = lax.axis_size("dom")
-    me = lax.axis_index("dom")
-    right, left = lax.rem(me + 1, count), lax.rem(me + count - 1, count)
-    greet("dom", [right, left])
-    copies = [
-        pltpu.make_async_remote_copy(
-            src_ref=first.at[:, pl.ds(start, 128)], dst_ref=edge, send_sem=send.at[i],
-            recv_sem=recv.at[i], device_id={"dom": other}, device_id_type=MESH,
-        )
-        for i, (start, edge, other) in enumerate(
-            ((slots - 128, low_edge, right), (0, high_edge, left))
-        )
-    ]
-    for copy in copies:
-        copy.start()
-    for copy in copies:
-        copy.wait()
-    low = jnp.where(me == 0, 0.0, low_edge[:, 127:128])
-    high = jnp.where(me == count - 1, 0.0, high_edge[:, 0:1])
-    lane = lax.broadcasted_iota(jnp.int32, (rows, slots), 1)
-    here = first[...]
-    below = jnp.where(lane == 0, jnp.broadcast_to(low, here.shape), pltpu.roll(here, 1, 1))
-    above = jnp.where(
-        lane == slots - 1, jnp.broadcast_to(high, here.shape), pltpu.roll(here, slots - 1, 1)
-    )
-    residual = rhs[...] + lateral[...] * (below + above)
-
-    def step(d):
-        out[d] = dot(residual, place_hot(places[...], cap, d), NT)
-
-    each(out.shape[0], step)
-
-
-def arrive_kernel(received, arrived, out, acc):
-    acc[...] = jnp.zeros_like(acc)
-    rows, line_dev = acc.shape
-
-    def step(d):
-        acc[...] += dot(received[d, :rows, :], line_hot(arrived[d], line_dev), NT)
-
-    each(received.shape[0], step)
-    quarter = out.shape[2]
-    for q in range(out.shape[0]):
-        out[q] = acc[:, q * quarter : (q + 1) * quarter]
-
-
-def reply_kernel(returned, arrived, out):
-    lines = jnp.concatenate([returned[q] for q in range(returned.shape[0])], axis=1)
-
-    def step(d):
-        out[d] = dot(lines, line_hot(arrived[d], lines.shape[1]), NN)
-
-    each(out.shape[0], step)
-
-
-def home_kernel(home, places, out):
-    out[...] = jnp.zeros_like(out)
-    cap = home.shape[2]
-
-    def step(d):
-        out[...] += dot(home[d], place_hot(places[...], cap, d), NN)
-
-    each(home.shape[0], step)
 
 
 def greet(axis, others):
@@ -399,6 +321,175 @@
     )(buffer)
 
 
+def is_dense(rows, cap):
+    return rows == 80 and cap == 96
+
+
+def block_shape(rows, cap):
+    return (64, 128) if is_dense(rows, cap) else (rows + 8, cap)
+
+
+def store_block(ref, d, block, rows):
+    cap = block.shape[1]
+    if not is_dense(rows, cap):
+        ref[d, : block.shape[0], :] = block
+        return
+    ref[d, :, :cap] = block[:64]
+    ref[d, 48:, cap:] = jnp.zeros((16, 32), jnp.float32)
+    for j in range(3):
+        ref[d, 16 * j : 16 * j + 16, cap:] = block[64:80, 32 * j : 32 * j + 32]
+        if block.shape[0] > rows:
+            ref[d, 48 + j : 49 + j, cap:] = block[80:81, 32 * j : 32 * j + 32]
+
+
+def load_block(ref, d, rows, cap):
+    if not is_dense(rows, cap):
+        return ref[d, :rows, :]
+    tail = jnp.concatenate([ref[d, 16 * j : 16 * j + 16, cap:] for j in range(3)], axis=1)
+    return jnp.concatenate([ref[d, :, :cap], tail], axis=0)
+
+
+def load_tags(ref, d, rows, cap):
+    if not is_dense(rows, cap):
+        return ref[d, rows : rows + 1, :]
+    return jnp.concatenate([ref[d, 48 + j : 49 + j, cap:] for j in range(3)], axis=1)
+
+
+def swap(bufs, make, use, rows):
+    sent, held, send, recv = bufs
+    count = sent.shape[0]
+    me = lax.axis_index("dom")
+
+    def copy(i, source, target, other):
+        return pltpu.make_async_remote_copy(
+            src_ref=sent.at[source], dst_ref=held.at[target], send_sem=send.at[i],
+            recv_sem=recv.at[i], device_id={"dom": other}, device_id_type=MESH,
+        )
+
+    def out(i):
+        other = lax.rem(me + i, count)
+        store_block(sent, other, make(other), rows)
+        copy(i, other, me, other).start()
+
+    def back(i):
+        other = lax.rem(me + count - i, count)
+        copy(i, other, other, other).wait_recv()
+        use(other)
+
+    def drain(i):
+        other = lax.rem(me + i, count)
+        copy(i, other, me, other).wait_send()
+
+    each(1, count, out)
+    store_block(held, me, make(me), rows)
+    use(me)
+    each(1, count, back)
+    each(1, count, drain)
+
+
+def partners(count):
+    me = lax.axis_index("dom")
+    return [lax.rem(me + i, count) for i in range(1, count)]
+
+
+def split_quarters(acc, out):
+    quarter = out.shape[2]
+    for q in range(out.shape[0]):
+        out[q] = acc[:, q * quarter : (q + 1) * quarter]
+
+
+def first_in_kernel(cap, rhs, ids, places, arrived, out, acc, *bufs):
+    rows, slots = rhs.shape
+    count = arrived.shape[0]
+    greet("dom", partners(count))
+    if slots & (slots - 1) == 0:
+        owner = lax.shift_right_logical(ids[...], slots.bit_length() - 1)
+    else:
+        owner = lax.div(ids[...], slots)
+    within = ids[...] - owner * slots
+    wide = max(count, 8)
+    mine = lax.broadcasted_iota(jnp.int32, (wide, slots), 0) == jnp.broadcast_to(owner, (wide, slots))
+    mine = mine.astype(jnp.float32)
+    shape = (slots, slots)
+    before = lax.broadcasted_iota(jnp.int32, shape, 0) < lax.broadcasted_iota(jnp.int32, shape, 1)
+    ahead = lax.dot_general(
+        mine, before.astype(jnp.float32), NN, preferred_element_type=jnp.float32
+    )
+    rank = jnp.sum(ahead * mine, axis=0, keepdims=True).astype(jnp.int32)
+    places[...] = owner * cap + rank
+    tags = jnp.broadcast_to((within + 1).astype(jnp.float32), (8, slots))
+    full = jnp.concatenate([rhs[...], tags], axis=0)
+    acc[...] = jnp.zeros_like(acc)
+
+    def make(d):
+        return dot(full, place_hot(places[...], cap, d), NT)
+
+    def use(d):
+        row = load_tags(bufs[1], d, rows, cap).astype(jnp.int32) - 1
+        arrived[d] = row
+        acc[...] += dot(load_block(bufs[1], d, rows, cap), line_hot(row, slots), NT)
+
+    swap(bufs, make, use, rows)
+    split_quarters(acc, out)
+
+
+def second_in_kernel(
+    cap, rhs, lateral, first, places, arrived, out, acc, low_edge, high_edge, edge_send, edge_recv, *bufs
+):
+    rows, slots = rhs.shape
+    count = arrived.shape[0]
+    me = lax.axis_index("dom")
+    right, left = lax.rem(me + 1, count), lax.rem(me + count - 1, count)
+    greet("dom", partners(count))
+    copies = [
+        pltpu.make_async_remote_copy(
+            src_ref=first.at[:, pl.ds(start, 128)], dst_ref=edge, send_sem=edge_send.at[i],
+            recv_sem=edge_recv.at[i], device_id={"dom": other}, device_id_type=MESH,
+        )
+        for i, (start, edge, other) in enumerate(
+            ((slots - 128, low_edge, right), (0, high_edge, left))
+        )
+    ]
+    for copy in copies:
+        copy.start()
+    acc[...] = jnp.zeros_like(acc)
+    for copy in copies:
+        copy.wait()
+    low = jnp.where(me == 0, 0.0, low_edge[:, 127:128])
+    high = jnp.where(me == count - 1, 0.0, high_edge[:, 0:1])
+    lane = lax.broadcasted_iota(jnp.int32, (rows, slots), 1)
+    here = first[...]
+    below = jnp.where(lane == 0, jnp.broadcast_to(low, here.shape), pltpu.roll(here, 1, 1))
+    above = jnp.where(
+        lane == slots - 1, jnp.broadcast_to(high, here.shape), pltpu.roll(here, slots - 1, 1)
+    )
+    residual = rhs[...] + lateral[...] * (below + above)
+
+    def make(d):
+        return dot(residual, place_hot(places[...], cap, d), NT)
+
+    def use(d):
+        acc[...] += dot(load_block(bufs[1], d, rows, cap), line_hot(arrived[d], slots), NT)
+
+    swap(bufs, make, use, rows)
+    split_quarters(acc, out)
+
+
+def home_kernel(cap, returned, arrived, places, out, *bufs):
+    rows, slots = out.shape
+    greet("dom", partners(arrived.shape[0]))
+    lines = jnp.concatenate([returned[q] for q in range(returned.shape[0])], axis=1)
+    out[...] = jnp.zeros_like(out)
+
+    def make(d):
+        return dot(lines, line_hot(arrived[d], slots), NN)
+
+    def use(d):
+        out[...] += dot(load_block(bufs[1], d, rows, cap), place_hot(places[...], cap, d), NN)
+
+    swap(bufs, make, use, rows)
+
+
 def body(rhs, lateral, piece_line, lower, diag_blocks, upper):
     fields, piece, line_dev = rhs.shape
     n_dom, n_sub = lax.axis_size("dom"), lax.axis_size("sub")
@@ -406,38 +497,40 @@
     cap = mean_load + (mean_load + 1) // 2
     rows = fields * piece
     f32 = lambda *shape: jax.ShapeDtypeStruct(shape, jnp.float32)
+    i32 = lambda *shape: jax.ShapeDtypeStruct(shape, jnp.int32)
     rhs = rhs.reshape(rows, line_dev)
     lateral = lateral.reshape(rows, line_dev)
-    owners = piece_line // line_dev
-    within = piece_line % line_dev
-    places, buffer = call(
-        functools.partial(pack_first_kernel, cap),
-        [jax.ShapeDtypeStruct((1, line_dev), jnp.int32), f32(n_dom, rows + 8, cap)],
-        rhs, owners, owners.reshape(line_dev, 1), within,
-    )
-    received = exchange(buffer, "dom", 0)
+    acc = pltpu.VMEM((rows, line_dev), jnp.float32)
+    bufs = [pltpu.VMEM((n_dom,) + block_shape(rows, cap), jnp.float32)] * 2
+    bufs += [pltpu.SemaphoreType.DMA((n_dom,))] * 2
+    quarters = f32(n_sub, rows, line_dev // n_sub)
+
+    def remote(number):
+        return pltpu.CompilerParams(
+            vmem_limit_bytes=40 * 1024 * 1024, collective_id=number, has_side_effects=True
+        )
+
     fac = factor(lower, diag_blocks, upper)
-    arrived = received[:, rows : rows + 1, :].astype(jnp.int32) - 1
-
-    def finish(received):
-        quarters = call(
-            arrive_kernel, f32(n_sub, rows, line_dev // n_sub), received, arrived,
-            scratch=[pltpu.VMEM((rows, line_dev), jnp.float32)],
-        )
-        solved = solve(fac, exchange(quarters, "sub", 2))
-        reply = call(reply_kernel, f32(n_dom, rows, cap), exchange(solved, "sub", 2), arrived)
-        return call(home_kernel, f32(rows, line_dev), exchange(reply, "dom", 1), places)
-
-    first = finish(received)
-    second = call(
-        functools.partial(pack_second_kernel, cap), f32(n_dom, rows, cap),
-        rhs, lateral, first, places,
-        scratch=[pltpu.VMEM((rows, 128), jnp.float32)] * 2 + [pltpu.SemaphoreType.DMA((2,))] * 2,
-        params=pltpu.CompilerParams(
-            vmem_limit_bytes=40 * 1024 * 1024, collective_id=3, has_side_effects=True
-        ),
-    )
-    return finish(exchange(second, "dom", 1)).reshape(fields, piece, line_dev)
+    places, arrived, sorted_first = call(
+        functools.partial(first_in_kernel, cap),
+        [i32(1, line_dev), i32(n_dom, 1, cap), quarters],
+        rhs, piece_line, scratch=[acc] + bufs, params=remote(0),
+    )
+
+    def finish(given):
+        solved = solve(fac, exchange(given, "sub", 2))
+        return call(
+            functools.partial(home_kernel, cap), f32(rows, line_dev),
+            exchange(solved, "sub", 2), arrived, places, scratch=bufs, params=remote(4),
+        )
+
+    first = finish(sorted_first)
+    edges = [pltpu.VMEM((rows, 128), jnp.float32)] * 2 + [pltpu.SemaphoreType.DMA((2,))] * 2
+    sorted_second = call(
+        functools.partial(second_in_kernel, cap), quarters, rhs, lateral, first, places, arrived,
+        scratch=[acc] + edges + bufs, params=remote(1),
+    )
+    return finish(sorted_second).reshape(fields, piece, line_dev)
 
 
 def solution(mesh):

time: 95.1 us -> 82.3 us (0.87)
  Pallas kernels: 88.7 us -> 76.2 us
  other arithmetic: 1.39 us -> 0 us
  local copies, waits for them, and re-layouts: 4.5 us -> 5.71 us
    pallas_call x8 -> x4, Pallas kernels: 63.3 us -> 18.4 us  [exchange(): pl.pallas_call(functools.partial(exchange_kernel, axis), out_shape=jax.Sh...]
    pallas_call x11 -> x7, Pallas kernels: 25.3 us -> 57.8 us  [call(): pl.pallas_call(kernel, out_shape=outs, in_specs=[space] * len(args), out_...]
    select_n x2 -> x0, other arithmetic: 1.39 us -> none  [the longest x1 0.7 us: body(): owners = piece_line // line_dev]
    unnamed x12 -> x15, local copies, waits for them, and re-layouts: 4.36 us -> 5.71 us
where the time goes in v2:
time: 82.3 us; the launch traced here: 82 us
  Pallas kernels  76.2 us (93%)
  local copies, waits for them, and re-layouts  5.71 us (7%)
    pallas_call x7, Pallas kernels, call(): pl.pallas_call(kernel, out_shape=outs, in_specs=[space] * len(args), out_...  57.8 us
    pallas_call x4, Pallas kernels, exchange(): pl.pallas_call(functools.partial(exchange_kernel, axis), out_shape=jax.Sh...  18.4 us
    unnamed x15, local copies, waits for them, and re-layouts  5.71 us

profile of v2, /device:TPU:0, one launch (start us, length us, event | category | flops | bytes accessed | tf_op | source)
XLA Modules:
  0.0 82.0 jit_solution(8510617685942452109)
XLA Ops:
  0.0 0.0 copy-start.3
  0.0 0.9 %copy-done.3 = f32[5,16,512]{2,1,0:T(8,128)S(1)} copy-done((f32[5,16,512]{2,1,0:T(8,128)S(1)}, f32[5,16,512]{2,1,0:T(8,128)}, u32[]{:S(2)}) %copy-start.3) | copy-done | bytes 163864
  0.9 0.0 copy-start.6
  0.9 0.7 copy-done.6
  1.6 14.0 %shard_map.65 = (s32[1,512]{1,0:T(1,128)S(1)}, s32[8,1,96]{2,1,0:T(1,128)S(1)}, f32[4,80,128]{2,1,0:T(8,128)S(1)}) custom-call(f32[80,512]{1,0:T(8,128)S(1)} %bitcast.3, s32[1,512]{1,0:T(1,128)S(1)} %copy-done.6), custom_call_target="tpu_custom_call" | custom-call | tf_op jit(solution)/shard_map/pallas_call | solution.py:25
  15.6 4.7 %shard_map.66.given = f32[4,80,128]{2,1,0:T(8,128)S(1)} custom-call(f32[4,80,128]{2,1,0:T(8,128)S(1)} %get-tuple-element.8.given), custom_call_target="tpu_custom_call" | custom-call | tf_op jit(solution)/shard_map/pallas_call | solution.py:310
  20.3 0.0 copy-start
  20.3 1.1 %copy-done = f32[5,5,64,128]{3,2,1,0:T(8,128)S(1)} copy-done((f32[5,5,64,128]{3,2,1,0:T(8,128)S(1)}, f32[5,5,64,128]{3,2,1,0:T(8,128)}, u32[]{:S(2)}) %copy-start) | copy-done | bytes 819224
  21.4 1.1 %copy-done.1 = f32[5,5,64,128]{3,2,1,0:T(8,128)S(1)} copy-done((f32[5,5,64,128]{3,2,1,0:T(8,128)S(1)}, f32[5,5,64,128]{3,2,1,0:T(8,128)}, u32[]{:S(2)}) %copy-start.1) | copy-done | bytes 819224
  22.6 1.1 %copy-done.2 = f32[5,5,64,128]{3,2,1,0:T(8,128)S(1)} copy-done((f32[5,5,64,128]{3,2,1,0:T(8,128)S(1)}, f32[5,5,64,128]{3,2,1,0:T(8,128)}, u32[]{:S(2)}) %copy-start.2) | copy-done | bytes 819224
  23.7 3.4 %shard_map.64.fac = f32[5,5,336,128]{3,2,1,0:T(8,128)S(1)} custom-call(f32[5,5,64,128]{3,2,1,0:T(8,128)S(1)} %copy-done, f32[5,5,64,128]{3,2,1,0:T(8,128)S(1)} %copy-done.1, f32[5,5,64,128]{3,2,1,0:T(8,128)S(1)} %copy-done.2), custom_call_target="tpu_custom_call" | custom-call | tf_op jit(solution)/shard_map/pallas_call | solution.py:25
  27.1 0.0 copy-start.4
  27.1 0.0 copy-start.5
  27.1 0.4 shard_map.67.given
  27.5 4.5 %shard_map.68.returned = f32[4,80,128]{2,1,0:T(8,128)S(1)} custom-call(f32[4,80,128]{2,1,0:T(8,128)S(1)} %shard_map.67.given), custom_call_target="tpu_custom_call" | custom-call | tf_op jit(solution)/shard_map/pallas_call | solution.py:310
  32.0 11.8 %shard_map.69.first = f32[80,512]{1,0:T(8,128)S(1)} custom-call(f32[4,80,128]{2,1,0:T(8,128)S(1)} %shard_map.68.returned, s32[8,1,96]{2,1,0:T(1,128)S(1)} %get-tuple-element.9.arrived, s32[1,512]{1,0:T(1,128)S(1)} %get-tuple-element.10.places), custom_call_target="tpu_custom_call" | custom-call | tf_op jit(solution)/shard_map/pallas_call | solution.py:25
  43.8 0.0 copy-done.4
  43.9 0.0 copy-done.5
  43.9 16.9 %shard_map.70.given = f32[4,80,128]{2,1,0:T(8,128)S(1)} custom-call(f32[80,512]{1,0:T(8,128)S(1)} %bitcast.4, f32[80,512]{1,0:T(8,128)S(1)} %bitcast.6, f32[80,512]{1,0:T(8,128)S(1)} %shard_map.69.first, s32[1,512]{1,0:T(1,128)S(1)} %get-tuple-element.10.places, s32[8,1,96]{2,1,0:T(1,128)S(1)} %get-tuple-element.9.arrived), custom_call_target="tpu_custom_call" | custom-call | tf_op jit(solution)/shard_map/pallas_call | solution.py:25
  60.7 4.5 %shard_map.71.given = f32[4,80,128]{2,1,0:T(8,128)S(1)} custom-call(f32[4,80,128]{2,1,0:T(8,128)S(1)} %shard_map.70.given), custom_call_target="tpu_custom_call" | custom-call | tf_op jit(solution)/shard_map/pallas_call | solution.py:310
  65.2 0.4 shard_map.72.given
  65.7 4.7 %shard_map.73.returned = f32[4,80,128]{2,1,0:T(8,128)S(1)} custom-call(f32[4,80,128]{2,1,0:T(8,128)S(1)} %shard_map.72.given), custom_call_target="tpu_custom_call" | custom-call | tf_op jit(solution)/shard_map/pallas_call | solution.py:310
  70.4 10.9 %shard_map.74 = f32[80,512]{1,0:T(8,128)S(1)} custom-call(f32[4,80,128]{2,1,0:T(8,128)S(1)} %shard_map.73.returned, s32[8,1,96]{2,1,0:T(1,128)S(1)} %get-tuple-element.9.arrived, s32[1,512]{1,0:T(1,128)S(1)} %get-tuple-element.10.places), custom_call_target="tpu_custom_call" | custom-call | tf_op jit(solution)/shard_map/pallas_call | solution.py:25
  81.3 0.7 copy.8
  (2 shorter events, 0.0 us)
Async XLA Ops:
  0.0 0.9 %copy-start.3 = (f32[5,16,512]{2,1,0:T(8,128)S(1)}, f32[5,16,512]{2,1,0:T(8,128)}, u32[]{:S(2)}) copy-start(f32[5,16,512]{2,1,0:T(8,128)} %param.6) | copy-start | bytes 491524
  0.9 0.7 copy-start.6
  20.3 1.1 %copy-start = (f32[5,5,64,128]{3,2,1,0:T(8,128)S(1)}, f32[5,5,64,128]{3,2,1,0:T(8,128)}, u32[]{:S(2)}) copy-start(f32[5,5,64,128]{3,2,1,0:T(8,128)} %low.1) | copy-start | bytes 2457604
  21.4 1.1 %copy-start.1 = (f32[5,5,64,128]{3,2,1,0:T(8,128)S(1)}, f32[5,5,64,128]{3,2,1,0:T(8,128)}, u32[]{:S(2)}) copy-start(f32[5,5,64,128]{3,2,1,0:T(8,128)} %mid.1) | copy-start | bytes 2457604
  22.6 1.1 %copy-start.2 = (f32[5,5,64,128]{3,2,1,0:T(8,128)S(1)}, f32[5,5,64,128]{3,2,1,0:T(8,128)}, u32[]{:S(2)}) copy-start(f32[5,5,64,128]{3,2,1,0:T(8,128)} %high.1) | copy-start | bytes 2457604
  27.1 16.8 %copy-start.4 = (f32[5,16,512]{2,1,0:T(8,128)S(1)}, f32[5,16,512]{2,1,0:T(8,128)}, u32[]{:S(2)}) copy-start(f32[5,16,512]{2,1,0:T(8,128)} %param.6) | copy-start | bytes 491524
  27.1 16.8 %copy-start.5 = (f32[5,16,512]{2,1,0:T(8,128)S(1)}, f32[5,16,512]{2,1,0:T(8,128)}, u32[]{:S(2)}) copy-start(f32[5,16,512]{2,1,0:T(8,128)} %param.7) | copy-start | bytes 491524
